TPU v7x, 512 devices: a whole 4x8x8 slice. The times are simulated.
512 devices in a mesh: row: 32 (over z_lo, x, core), col: 16 (over z_hi, y).
Axes of the slice: x: 4, y: 8, z: 8 (z_hi: 2, z_lo: 4; z = z_hi * 4 + z_lo), core: 2. Of those that a mesh axis runs over, the one named last changes fastest.
Arguments:
- ingest: bfloat16 [8192, 32768], P(('row', 'col')), may hold values from -128 to 127, as said below
- row_order: int32 [32, 256], P('row'), may hold values from 0 to 255, each once within a row
- matrix_seeds: int32 [2], replicated, may hold values from 0 to 46336
Outputs:
- second_hint: float32 [4, 2, 1024, 1024], P(None, None, 'col')
Inputs may be any that keep to these rules, and one draw needn't show every extreme that they name: `ingest`: integers. `row_order`: each row is a permutation of 0 to 255.
All inputs are finite; a program needn't handle non-finite values.
Results may differ from a plain program's by a relative error of at most 0.0003.
Values may be sent and summed in bfloat16 or wider, within the bound.
A program may use at most 64 MiB of HBM per device.

v0:
```python
import functools

import jax
import jax.numpy as jnp
from jax import lax
from jax.experimental import pallas as pl
from jax.experimental.pallas import tpu as pltpu
from jax.sharding import PartitionSpec as P

PRIME = 46337
HALF = 23168
INV = 1.0 / PRIME
MAGIC_ONE = 1.5 * 2.0**23
MAGIC_BYTE = 1.5 * 2.0**31
BIAS = (HALF * 65537 - 0x80808080) % 2**32
BIAS = BIAS - 2**32 if BIAS >= 2**31 else BIAS
NEAR = ((0, 0, 0), (0, 1, 0), (1, 0, 0), (0, 0, 1), (0, 1, 1), (0, 0, -1), (-1, 0, 0), (0, -1, 0))
ORDER = (4, 1, 2, 3, 5, 6, 7, 0)
MESH = pl.DeviceIdType.MESH
F32, BF16, I32 = jnp.float32, jnp.bfloat16, jnp.int32
NT = (((1,), (1,)), ((), ()))
NN = (((1,), (0,)), ((), ()))


def modp(v):
    q = (v.astype(F32) * INV).astype(I32)
    r = v - q * PRIME
    r = jnp.where(r < 0, r + PRIME, r)
    return jnp.where(r >= PRIME, r - PRIME, r)


def centred(v):
    return jnp.where(v > HALF, v - PRIME, v)


def two_digits(v):
    hi = ((v + 128 + 65536) // 256 - 256) * 256
    return hi, v - hi


def pick_rows(rows, shape):
    at = lax.broadcasted_iota(I32, shape, 0)
    out = jnp.zeros(shape, I32)
    for k, row in enumerate(rows):
        out = jnp.where(at == k, row, out)
    return out.astype(F32)


def index_digits(index, seed):
    x = modp(modp(index * 40503) + seed)
    x = modp(x * x)
    hi, lo = two_digits(centred(modp(x * x)))
    nib = [lax.shift_right_logical(x, jnp.int32(4 * k)) & 15 for k in range(4)]
    one = jnp.ones_like(x)
    return pick_rows(nib + nib + [hi, lo, one, one], (16, index.shape[1]))


def column_digits(index):
    b = modp(index * 29989)
    his, los = [], []
    w = modp(b + b)
    for k in range(4):
        hi, lo = two_digits(centred(w))
        his.append(hi)
        los.append(lo)
        w = modp(w * 16)
    hi, lo = two_digits(centred(modp(modp(b * b) + (12345 - HALF + PRIME))))
    one = jnp.ones_like(b)
    return pick_rows(his + los + [one, one, hi, lo], (16, index.shape[1]))


def residue_digits(v):
    q = (v * INV + MAGIC_ONE) - MAGIC_ONE
    r = v - q * PRIME
    hi = (r + MAGIC_BYTE) - MAGIC_BYTE
    return (r - hi).astype(BF16), hi.astype(BF16)


def joined(parts):
    t = parts[0].astype(I32)
    t = t + lax.shift_left((parts[1] * (1.0 / 256)).astype(I32), jnp.int32(8))
    t = t + lax.shift_left(parts[2].astype(I32), jnp.int32(16))
    return t + lax.shift_left((parts[3] * (1.0 / 256)).astype(I32), jnp.int32(24))


def kernel(
    seeds, ingest, order, out,
    rec, orders, bdig, xdig, gen_a, gen_b, part, sib, red, hint_send, hint_in, a2, tot, xbuf, xsum, zbuf, full,
    s_in, r_in, s_ord, r_ord, s_sib, r_sib, s_red, r_red, s_hint, r_hint, s_x, r_x, s_z, r_z, s_gz, r_gz, s_gx, r_gx,
    s_gs, r_gs, s_out,
):
    row, col = lax.axis_index("row"), lax.axis_index("col")
    core, x, zl = row % 2, (row // 2) % 4, row // 8
    y, zh = col % 8, col // 8
    z = zh * 4 + zl

    def dev(dx, dy, dz, other):
        xx, yy, zz = (x + dx + 4) % 4, (y + dy + 8) % 8, (z + dz + 8) % 8
        cc = (core + other) % 2
        return {"row": ((zz % 4) * 4 + xx) * 2 + cc, "col": (zz // 4) * 8 + yy}

    def dev_line(dz):
        return {"row": (((zl + dz) % 4) * 4 + x) * 2 + core, "col": col}

    def rcopy(src, dst, ssem, rsem, device):
        return pltpu.make_async_remote_copy(
            src_ref=src, dst_ref=dst, send_sem=ssem, recv_sem=rsem, device_id=device, device_id_type=MESH
        )

    sibling = dev(0, 0, 0, 1)

    barrier = pltpu.get_barrier_semaphore()

    def greet(device):
        pl.semaphore_signal(barrier, inc=1, device_id=device, device_id_type=MESH)

    count = 0
    for off in ((1, 0, 0), (-1, 0, 0), (0, 0, 1), (0, 0, -1), (0, 1, 1), (0, -1, -1)):
        for other in range(2):
            greet(dev(*off, other))
            count += 1
    greet(dev(2, 0, 0, 0))
    count += 1
    for dz in range(1, 4):
        greet(dev_line(dz))
        count += 1

    def greet_col(k, carry):
        greet({"row": row - core + (core + k) % 2, "col": (col + k // 2) % 16})
        return carry

    lax.fori_loop(1, 32, greet_col, 0)
    pl.semaphore_wait(barrier, count + 31)

    colour = (2 * x + y + 3 * z) % 8

    def ingest_src(near, other):
        return ingest.at[:, pl.ds(((colour + near) % 8) * 4096 + ((core + other) % 2) * 2048, 2048)]

    def ingest_copy(near, other):
        slot = near * 2 + core
        return rcopy(
            ingest_src(near, other), rec.at[pl.ds(slot * 16, 16), :],
            s_in.at[near * 2 + other], r_in.at[slot], dev(*NEAR[near], other),
        )

    for near in ORDER:
        for other in range(2):
            if near or other:
                ingest_copy(near, other).start()
    own_in = pltpu.make_async_copy(ingest_src(0, 0), rec.at[pl.ds(core * 16, 16), :], r_in.at[core])
    own_in.start()
    orders[core] = jnp.broadcast_to(order[...], (8, 256))
    order_copy = rcopy(orders.at[core], orders.at[core], s_ord, r_ord, sibling)
    order_copy.start()

    bdig[...] = jnp.transpose(column_digits(lax.broadcasted_iota(I32, (1, 1024), 1))).astype(BF16)
    col_start = colour * 4096 + core * 2048
    index = lax.broadcasted_iota(I32, (1, 2048), 1) + col_start
    for w in range(2):
        xdig[w] = index_digits(index, seeds[0] + 7919 * w).astype(BF16)

    rcopy(orders.at[1 - core], orders.at[1 - core], s_ord, r_ord, sibling).wait_recv()

    half = pl.ds(pl.multiple_of(core * 512, 512), 512)
    for blk in range(2):
        rows_i = (row - core + blk) * 256 + lax.broadcasted_iota(I32, (1, 256), 1)
        onehot = (lax.broadcasted_iota(I32, (256, 256), 0) == orders[blk, 0:1, :]).astype(F32).astype(BF16)
        for w in range(2):
            dig = index_digits(rows_i, seeds[1] + 7919 * w).astype(BF16)
            perm = lax.dot_general(onehot, dig, NT, preferred_element_type=F32).astype(BF16)
            v = lax.dot_general(perm, bdig[half, :], NT, preferred_element_type=F32)
            lo, hi = residue_digits(v)
            a2[2 * w, blk * 256 : (blk + 1) * 256, :] = lo
            a2[2 * w + 1, blk * 256 : (blk + 1) * 256, :] = hi

    def generate(buf, t, kh):
        n_at = pl.multiple_of((((1 - core) * 2 + t) % 4) * 256, 256)
        left = bdig[pl.ds(n_at, 256), :]
        for w in range(2):
            v = lax.dot_general(left, xdig[w, :, kh * 1024 : (kh + 1) * 1024], NN, preferred_element_type=F32)
            lo, hi = residue_digits(v)
            buf[(2 * w) * 256 : (2 * w + 1) * 256, :] = lo
            buf[(2 * w + 1) * 256 : (2 * w + 2) * 256, :] = hi

    def multiply(buf, kh):
        r = lax.dot_general(buf[...], rec[:, kh * 1024 : (kh + 1) * 1024], NT, preferred_element_type=F32)
        return joined([r[k * 256 : (k + 1) * 256, :] for k in range(4)])

    generate(gen_a, 0, 0)
    for slot in range(16):
        rcopy(
            rec.at[pl.ds(slot * 16, 16), :], rec.at[pl.ds(slot * 16, 16), :], s_in.at[0], r_in.at[slot], sibling
        ).wait_recv()
    sums = lax.dot_general(jnp.ones((16, 2048), BF16), rec[...], NT, preferred_element_type=F32)
    bias = sums[0:1, :].astype(I32) * jnp.int32(BIAS)

    sib_copy = rcopy(part.at[1 - core], sib, s_sib, r_sib, sibling)

    def tile(t, carry):
        generate(gen_b, t, 1)
        acc = multiply(gen_a, 0)
        generate(gen_a, t + 1, 0)
        acc = acc + multiply(gen_b, 1) + bias
        part[(1 - core + t // 2) % 2, :, pl.ds(pl.multiple_of((t % 2) * 256, 256), 256)] = jnp.transpose(acc)

        @pl.when(t == 1)
        def _():
            sib_copy.start()

        return carry

    lax.fori_loop(0, 4, tile, 0)
    sib_copy.wait_recv()
    mine = part.at[core]
    mine[...] = mine[...] + sib[...]

    def red_copy(near):
        dx, dy, dz = NEAR[near]
        return rcopy(
            mine.at[pl.ds(near * 32, 32), :], red.at[near], s_red.at[near], r_red.at[near], dev(-dx, -dy, -dz, 0)
        )

    for near in ORDER[:-1]:
        red_copy(near).start()
    hint = mine[0:32, :]
    for near in range(1, 8):
        red_copy(near).wait_recv()
        hint = hint + red[near]

    low_lane = lax.broadcasted_iota(I32, (16, 128), 1) < 64
    for t in range(4):
        top, low = hint[0:16, t * 128 : (t + 1) * 128], hint[16:32, t * 128 : (t + 1) * 128]
        hint_send[2 * t] = jnp.where(low_lane, top, pltpu.roll(low, 64, 1))
        hint_send[2 * t + 1] = jnp.where(low_lane, pltpu.roll(top, 64, 1), low)
    landing = hint_in.at[pl.ds(col * 16, 16), :]
    local = zh == core

    def hint_copy(dy, other):
        yy = (y + dy) % 8
        return rcopy(
            hint_send.at[yy], landing, s_hint.at[dy * 2 + other], r_hint.at[col],
            {"row": row - core + (core + other) % 2, "col": core * 8 + yy},
        )

    own_hint = pltpu.make_async_copy(hint_send.at[y], landing, r_hint.at[col])
    for dy in (4, 3, 5, 2, 6, 1, 7, 0):
        for other in range(2):
            if dy or other:
                hint_copy(dy, other).start()
            else:
                @pl.when(local)
                def _():
                    own_hint.start()

                @pl.when(jnp.logical_not(local))
                def _():
                    hint_copy(0, 0).start()

    for c in range(16):
        spot = hint_in.at[pl.ds(c * 16, 16), :]
        rcopy(spot, spot, s_hint.at[0], r_hint.at[c], sibling).wait_recv()

    turned = jnp.transpose(hint_in[...])
    wide = jnp.concatenate([turned[0:64, :], turned[64:128, :]], axis=1)
    left = jnp.concatenate(
        [
            ((lax.shift_right_logical(wide, jnp.int32(8 * d)) & 255) - 128).astype(F32).astype(BF16)
            for d in range(4)
        ],
        axis=0,
    )
    lsum = lax.dot_general(left, jnp.ones((512, 128), BF16), NN, preferred_element_type=F32)
    lbias = lsum[:, 0:1].astype(I32) * jnp.int32(BIAS)
    tot[...] = joined([lax.dot_general(left, a2[k], NN, preferred_element_type=F32) for k in range(4)]) + lbias

    def x_copy(dx):
        xx = (x + dx) % 4
        return rcopy(tot.at[pl.ds(xx * 64, 64), :], xbuf.at[dx - 1], s_x.at[dx - 1], r_x.at[dx - 1], dev(dx, 0, 0, 0))

    def z_copy(dz):
        zz = (zl + dz) % 4
        return rcopy(xsum.at[pl.ds(zz * 16, 16), :], zbuf.at[dz - 1], s_z.at[dz - 1], r_z.at[dz - 1], dev_line(dz))

    for dx in (2, 1, 3):
        x_copy(dx).start()
    acc = tot[pl.ds(pl.multiple_of(x * 64, 64), 64), :]
    for dx in (1, 3, 2):
        x_copy(dx).wait_recv()
        acc = acc + xbuf[dx - 1]
    xsum[...] = acc
    for dz in (1, 3, 2):
        z_copy(dz).start()
    acc = xsum[pl.ds(pl.multiple_of(zl * 16, 16), 16), :]
    for dz in (1, 3, 2):
        z_copy(dz).wait_recv()
        acc = acc + zbuf[dz - 1]

    full[core, pl.ds(pl.multiple_of(x * 64 + zl * 16, 16), 16), :] = acc

    def gz_copy(dz, source):
        spot = full.at[core, pl.ds(x * 64 + source * 16, 16), :]
        return rcopy(spot, spot, s_gz.at[dz - 1], r_gz.at[dz - 1], dev_line(dz))

    def gx_copy(dx, source):
        spot = full.at[core, pl.ds(source * 64, 64), :]
        return rcopy(spot, spot, s_gx.at[dx - 1], r_gx.at[dx - 1], dev(dx, 0, 0, 0))

    def gs_copy(dx, half_at):
        spot = full.at[half_at, pl.ds(((x + 4 - dx) % 4) * 64, 64), :]
        return rcopy(spot, spot, s_gs.at[dx], r_gs.at[dx], sibling)

    for dz in (1, 3, 2):
        gz_copy(dz, zl).start()
    for dz in (1, 3, 2):
        gz_copy(dz, (zl + 4 - dz) % 4).wait_recv()
    for dx in (2, 1, 3):
        gx_copy(dx, x).start()
    gs_copy(0, core).start()
    for dx in (1, 3, 2):
        gx_copy(dx, (x + 4 - dx) % 4).wait_recv()
        gs_copy(dx, core).start()
    for dx in (0, 1, 3, 2):
        gs_copy(dx, 1 - core).wait_recv()
    result = pltpu.make_async_copy(full, out, s_out)
    result.start()

    for near in range(8):
        for other in range(2):
            if near or other:
                ingest_copy(near, other).wait_send()
    order_copy.wait_send()
    sib_copy.wait_send()
    for near in range(1, 8):
        red_copy(near).wait_send()
    for dy in range(8):
        for other in range(2):
            if dy or other:
                hint_copy(dy, other).wait_send()
            else:
                @pl.when(jnp.logical_not(local))
                def _():
                    hint_copy(0, 0).wait_send()
    for d in range(1, 4):
        x_copy(d).wait_send()
        z_copy(d).wait_send()
        gz_copy(d, zl).wait_send()
        gx_copy(d, x).wait_send()
    for d in range(4):
        gs_copy(d, core).wait_send()
    result.wait()


def on_device(ingest, row_order, matrix_seeds):
    dma = pltpu.SemaphoreType.DMA
    scratch = [
        pltpu.VMEM((256, 2048), BF16),
        pltpu.VMEM((2, 8, 256), I32),
        pltpu.VMEM((1024, 16), BF16),
        pltpu.VMEM((2, 16, 2048), BF16),
        pltpu.VMEM((1024, 1024), BF16),
        pltpu.VMEM((1024, 1024), BF16),
        pltpu.VMEM((2, 256, 512), I32),
        pltpu.VMEM((256, 512), I32),
        pltpu.VMEM((8, 32, 512), I32),
        pltpu.VMEM((8, 16, 128), I32),
        pltpu.VMEM((256, 128), I32),
        pltpu.VMEM((4, 512, 512), BF16),
        pltpu.VMEM((256, 512), I32),
        pltpu.VMEM((3, 64, 512), I32),
        pltpu.VMEM((64, 512), I32),
        pltpu.VMEM((3, 16, 512), I32),
        pltpu.VMEM((2, 256, 512), I32),
        dma((16,)), dma((16,)), dma, dma, dma, dma, dma((8,)), dma((8,)), dma((16,)), dma((16,)),
        dma((3,)), dma((3,)), dma((3,)), dma((3,)), dma((3,)), dma((3,)), dma((3,)), dma((3,)),
        dma((4,)), dma((4,)), dma,
    ]
    total = pl.pallas_call(
        kernel,
        out_shape=jax.ShapeDtypeStruct((2, 256, 512), I32),
        in_specs=[
            pl.BlockSpec(memory_space=pltpu.SMEM),
            pl.BlockSpec(memory_space=pl.ANY),
            pl.BlockSpec(memory_space=pltpu.VMEM),
        ],
        out_specs=pl.BlockSpec(memory_space=pl.ANY),
        scratch_shapes=scratch,
        compiler_params=pltpu.CompilerParams(
            collective_id=0, has_side_effects=True, vmem_limit_bytes=48 * 2**20
        ),
        name="hints",
    )(matrix_seeds, ingest, row_order)
    total = jnp.transpose(total.reshape(2, 4, 64, 512), (1, 2, 0, 3)).reshape(4, 64, 1024)
    low = (total & 65535).astype(F32)
    high = lax.shift_right_logical(total, jnp.int32(16)).astype(F32)
    return jnp.stack([low, high], axis=1) * (1.0 / 65536.0)


def solution(mesh):
    return jax.shard_map(
        on_device, mesh=mesh,
        in_specs=(P(("row", "col"), None), P("row", None), P()),
        out_specs=P(None, None, "col", None), check_vma=False,
    )
```

profile of v0, /device:TPU:1, one launch (start us, length us, event | category | flops | bytes accessed | tf_op | source)
XLA Modules:
  0.0 83.4 jit_solution(7864911023008084786)
XLA Ops:
  0.0 0.0 copy-start
  0.0 1.2 %copy-done = bf16[16,32768]{1,0:T(8,128)(2,1)S(1)} copy-done((bf16[16,32768]{1,0:T(8,128)(2,1)S(1)}, bf16[16,32768]{1,0:T(8,128)(2,1)}, u32[]{:S(2)}) %copy-start) | copy-done | bytes 1048600
  1.2 0.0 copy-start.1
  1.2 0.7 copy-done.1
  1.9 0.0 copy-start.2
  1.9 0.7 copy-done.2
  2.6 75.8 %hints.1 = s32[2,256,512]{2,1,0:T(8,128)S(1)} custom-call(s32[2]{0:T(128)S(1)} %copy-done.2, bf16[16,32768]{1,0:T(8,128)(2,1)S(1)} %copy-done, s32[1,256]{1,0:T(1,128)S(1)} %copy-done.1), custom_call_target="tpu_custom_call" | custom-call | tf_op jit(solution)/shard_map/hints/pallas_call | solution.py:378
  78.3 0.2 and_convert_fusion
  78.5 0.8 copy.4
  79.3 0.9 %convert_element_type.41 = f32[4,1,64,1024]{3,2,1,0:T(8,128)S(1)} reshape(f32[4,64,2,512]{3,2,1,0:T(2,128)S(1)} %copy.4) | data formatting | bytes 2097152 | tf_op jit(solution)/shard_map/convert_element_type | solution.py:394
  80.2 0.8 copy.5
  81.0 0.9 %convert_element_type.45 = f32[4,1,64,1024]{3,2,1,0:T(8,128)S(1)} reshape(f32[4,64,2,512]{3,2,1,0:T(2,128)S(1)} %copy.5) | data formatting | bytes 2097152 | tf_op jit(solution)/shard_map/convert_element_type | solution.py:395
  81.9 1.5 %maximum_multiply_fusion = f32[4,2,64,1024]{3,2,1,0:T(8,128)} fusion(f32[4,1,64,1024]{3,2,1,0:T(8,128)S(1)} %convert_element_type.45, f32[4,1,64,1024]{3,2,1,0:T(8,128)S(1)} %convert_element_type.41), kind=kLoop, calls=%fused_computation | loop fusion | flops 1048576 | bytes 4194304 | tf_op jit(solution)/shard_map/mul | solution.py:396
Async XLA Ops:
  0.0 1.2 %copy-start = (bf16[16,32768]{1,0:T(8,128)(2,1)S(1)}, bf16[16,32768]{1,0:T(8,128)(2,1)}, u32[]{:S(2)}) copy-start(bf16[16,32768]{1,0:T(8,128)(2,1)} %ingest.1) | copy-start | bytes 3145732
  1.2 0.7 copy-start.1
  1.9 0.7 copy-start.2
where the time goes:
time: 83.6 us; the launch traced here: 83.4 us
  Pallas kernels  75.8 us (91%)
  local copies, waits for them, and re-layouts  5.98 us (7%)
  other arithmetic  1.65 us (2%)
    pallas_call x1, Pallas kernels, on_device(): pl.pallas_call(kernel, out_shape=jax.ShapeDtypeStruct((2, 256, 512), I32)...  75.8 us
    unnamed x6, local copies, waits for them, and re-layouts  2.56 us
    convert_element_type x2, local copies, waits for them, and re-layouts, on_device(): high = lax.shift_right_logical(total, jnp.int32(16)).astype(F32)  1.71 us
    convert_element_type x2, local copies, waits for them, and re-layouts, on_device(): low = (total & 65535).astype(F32)  1.71 us

commit v1 on v0

v1 whole, which is shorter than its diff:
```python
import functools

import jax
import jax.numpy as jnp
from jax import lax
from jax.experimental import pallas as pl
from jax.experimental.pallas import tpu as pltpu
from jax.sharding import PartitionSpec as P

PRIME = 46337
HALF = 23168
INV = 1.0 / PRIME
MAGIC_ONE = 1.5 * 2.0**23
MAGIC_BYTE = 1.5 * 2.0**31
BIAS = (HALF * 65537 - 0x80808080) % 2**32
BIAS = BIAS - 2**32 if BIAS >= 2**31 else BIAS
NEAR = ((0, 0, 0), (0, 1, 0), (1, 0, 0), (0, 0, 1), (0, 1, 1), (0, 0, -1), (-1, 0, 0), (0, -1, 0))
ORDER = (4, 1, 2, 3, 5, 6, 7, 0)
MESH = pl.DeviceIdType.MESH
F32, BF16, I32 = jnp.float32, jnp.bfloat16, jnp.int32
NT = (((1,), (1,)), ((), ()))
NN = (((1,), (0,)), ((), ()))


def modp(v):
    q = (v.astype(F32) * INV).astype(I32)
    r = v - q * PRIME
    r = jnp.where(r < 0, r + PRIME, r)
    return jnp.where(r >= PRIME, r - PRIME, r)


def centred(v):
    return jnp.where(v > HALF, v - PRIME, v)


def two_digits(v):
    hi = ((v + 128 + 65536) // 256 - 256) * 256
    return hi, v - hi


def pick_rows(rows, shape):
    at = lax.broadcasted_iota(I32, shape, 0)
    out = jnp.zeros(shape, I32)
    for k, row in enumerate(rows):
        out = jnp.where(at == k, row, out)
    return out.astype(F32)


def index_digits(index, seed):
    x = modp(modp(index * 40503) + seed)
    x = modp(x * x)
    hi, lo = two_digits(centred(modp(x * x)))
    nib = [lax.shift_right_logical(x, jnp.int32(4 * k)) & 15 for k in range(4)]
    one = jnp.ones_like(x)
    return pick_rows(nib + nib + [hi, lo, one, one], (16, index.shape[1]))


def column_digits(index):
    b = modp(index * 29989)
    his, los = [], []
    w = modp(b + b)
    for k in range(4):
        hi, lo = two_digits(centred(w))
        his.append(hi)
        los.append(lo)
        w = modp(w * 16)
    hi, lo = two_digits(centred(modp(modp(b * b) + (12345 - HALF + PRIME))))
    one = jnp.ones_like(b)
    return pick_rows(his + los + [one, one, hi, lo], (16, index.shape[1]))


def residue_digits(v):
    q = (v * INV + MAGIC_ONE) - MAGIC_ONE
    r = v - q * PRIME
    hi = (r + MAGIC_BYTE) - MAGIC_BYTE
    return (r - hi).astype(BF16), hi.astype(BF16)


def joined(parts):
    t = parts[0].astype(I32)
    t = t + lax.shift_left((parts[1] * (1.0 / 256)).astype(I32), jnp.int32(8))
    t = t + lax.shift_left(parts[2].astype(I32), jnp.int32(16))
    return t + lax.shift_left((parts[3] * (1.0 / 256)).astype(I32), jnp.int32(24))


def kernel(
    seeds, ingest, order, out,
    rec, order_in, orders, bdig, xdig, xdig2, gen_a, gen_b, give, sib, mine, red, hint_send, hall, a2,
    tot, tsib, zbuf, full,
    s_in, r_in, s_own, s_ord, r_ord, s_sib, r_sib, s_red, r_red, s_hint, r_hint, s_hx, r_hx, s_tot, r_tot,
    s_z, r_z, s_gz, r_gz, s_gx, r_gx, s_gs, r_gs, s_out,
):
    row, col = lax.axis_index("row"), lax.axis_index("col")
    core, x, zl = row % 2, (row // 2) % 4, row // 8
    y, zh = col % 8, col // 8
    z = zh * 4 + zl

    def dev_at(xx, yy, zz, cc):
        return {"row": ((zz % 4) * 4 + xx) * 2 + cc, "col": (zz // 4) * 8 + yy}

    def dev(dx, dy, dz, other):
        return dev_at((x + dx + 4) % 4, (y + dy + 8) % 8, (z + dz + 8) % 8, (core + other) % 2)

    def dev_line(dz):
        return dev_at(x, y, zh * 4 + (zl + dz) % 4, core)

    def rcopy(src, dst, ssem, rsem, device):
        return pltpu.make_async_remote_copy(
            src_ref=src, dst_ref=dst, send_sem=ssem, recv_sem=rsem, device_id=device, device_id_type=MESH
        )

    sibling = dev(0, 0, 0, 1)

    def arrived(spot, rsem):
        rcopy(spot, spot, s_tot, rsem, sibling).wait_recv()

    order_load = pltpu.make_async_copy(order, order_in, s_own)
    order_load.start()

    barrier = pltpu.get_barrier_semaphore()

    def greet(device):
        pl.semaphore_signal(barrier, inc=1, device_id=device, device_id_type=MESH)

    def greet_plane(k, carry):
        side = k // 16
        zz = z + side * (7 - 2 * z)
        greet(dev_at(x, (y + (k // 2) % 8) % 8, zz, (core + k) % 2))
        return carry

    lax.fori_loop(1, 32, greet_plane, 0)
    count = 31
    for off in ((1, 0, 0), (-1, 0, 0), (0, 0, 1), (0, 0, -1), (0, 1, 1), (0, -1, -1)):
        for other in range(2):
            greet(dev(*off, other))
            count += 1
    greet(dev(2, 0, 0, 0))
    for d in range(1, 4):
        greet(dev_line(d))
        greet(dev_at((x + d) % 4, y, 7 - z, core))
    pl.semaphore_wait(barrier, count + 7)

    colour = (2 * x + y + 3 * z) % 8
    sign = 1 - 2 * core

    def ingest_src(near, other):
        return ingest.at[:, pl.ds(((colour + near) % 8) * 4096 + ((core + other) % 2) * 2048, 2048)]

    def ingest_copy(near, other):
        slot = near * 2 + core
        device = dev(0, sign, sign, other) if near == 4 else dev(*NEAR[near], other)
        return rcopy(
            ingest_src(near, other), rec.at[pl.ds(slot * 16, 16), :],
            s_in.at[near * 2 + other], r_in.at[slot], device,
        )

    for near in ORDER:
        for other in range(2):
            if near or other:
                ingest_copy(near, other).start()
    own_in = pltpu.make_async_copy(ingest_src(0, 0), rec.at[pl.ds(core * 16, 16), :], r_in.at[core])
    own_in.start()

    order_load.wait()
    orders[0, 0] = jnp.broadcast_to(order_in[...], (8, 256))

    def order_copy(k):
        side, dx = k // 4, k % 4
        zz = 7 - z if side else z
        return rcopy(
            orders.at[0, 0], orders.at[side, dx], s_ord.at[k], r_ord.at[k], dev_at((x + dx) % 4, y, zz, core)
        )

    for k in range(1, 8):
        order_copy(k).start()

    bdig[...] = jnp.transpose(column_digits(lax.broadcasted_iota(I32, (1, 1024), 1))).astype(BF16)
    lane = lax.broadcasted_iota(I32, (1, 2048), 1)
    mirrored = (lane // 256) % 2
    block = ((zl + mirrored * (3 - 2 * zl)) * 4 + (x + 4 - lane // 512) % 4) * 2 + core
    for w in range(2):
        xdig[w] = index_digits(lane + (colour * 4096 + core * 2048), seeds[0] + 7919 * w).astype(BF16)
        xdig2[w] = index_digits(block * 256 + lane % 256, seeds[1] + 7919 * w).astype(BF16)

    def generate(buf, t, kh):
        n_at = pl.multiple_of((((1 - core) * 2 + t) % 4) * 256, 256)
        left = bdig[pl.ds(n_at, 256), :]
        for w in range(2):
            digits = xdig[w, :, kh * 1024 : (kh + 1) * 1024]
            lo, hi = residue_digits(lax.dot_general(left, digits, NN, preferred_element_type=F32))
            buf[(2 * w) * 256 : (2 * w + 1) * 256, :] = lo
            buf[(2 * w + 1) * 256 : (2 * w + 2) * 256, :] = hi

    def multiply(buf, kh):
        r = lax.dot_general(buf[...], rec[:, kh * 1024 : (kh + 1) * 1024], NT, preferred_element_type=F32)
        return joined([r[k * 256 : (k + 1) * 256, :] for k in range(4)])

    def ahead(t, carry):
        for kh in range(2):
            generate(gen_a.at[t * 2 + kh], t, kh)
        return carry

    lax.fori_loop(0, 2, ahead, 0)

    for k in range(1, 8):
        arrived(orders.at[k // 4, k % 4], r_ord.at[k])
    spot = lax.broadcasted_iota(I32, (256, 1), 0)
    side = (spot // 64) % 2
    ingest_row = ((zh + side * (1 - 2 * zh)) * 8 + (spot // 8) % 8) * 16 + (spot // 128) * 8 + spot % 8
    wanted = ingest_row + 256 * side
    lane = lax.broadcasted_iota(I32, (1, 512), 1)
    quarter = bdig[pl.ds(pl.multiple_of(x * 256, 256), 256), :]
    for dx in range(4):
        have = jnp.concatenate([orders[0, dx, 0:1, :], orders[1, dx, 0:1, :]], axis=1) + (lane // 256) * 256
        onehot = (wanted == have).astype(F32).astype(BF16)
        for w in range(2):
            digits = xdig2[w, :, dx * 512 : (dx + 1) * 512]
            perm = lax.dot_general(onehot, digits, NT, preferred_element_type=F32).astype(BF16)
            lo, hi = residue_digits(lax.dot_general(perm, quarter, NT, preferred_element_type=F32))
            a2[2 * w, dx * 256 : (dx + 1) * 256, :] = lo
            a2[2 * w + 1, dx * 256 : (dx + 1) * 256, :] = hi

    for slot in range(16):
        arrived(rec.at[pl.ds(slot * 16, 16), :], r_in.at[slot])
    sums = lax.dot_general(jnp.ones((16, 2048), BF16), rec[...], NT, preferred_element_type=F32)
    bias = sums[0:1, :].astype(I32) * jnp.int32(BIAS)

    def tile(t, carry):
        acc = bias
        for kh in range(2):
            generate(gen_b.at[t * 2 + kh], t + 2, kh)
            acc = acc + multiply(gen_a.at[t * 2 + kh], kh)
        give[t] = jnp.transpose(acc)
        return carry

    lax.fori_loop(0, 2, tile, 0)
    sib_copy = rcopy(give, sib, s_sib, r_sib, sibling)
    sib_copy.start()

    def red_copy(q, near):
        if near in (4, 8):
            at, sg = (near // 4 - 1) * 16, 1 if near == 8 else -1
            rows, dst, device = 128 + at, red.at[q, 4, pl.ds(at, 16), :], dev(0, sg, sg, 0)
            rows = mine.at[q, pl.ds(rows, 16), :]
        else:
            dx, dy, dz = NEAR[near]
            rows, dst, device = mine.at[q, pl.ds(near * 32, 32), :], red.at[q, near], dev(-dx, -dy, -dz, 0)
        return rcopy(rows, dst, s_red.at[q * 9 + near], r_red.at[q * 9 + near], device)

    for q in range(2):
        acc = bias
        for kh in range(2):
            acc = acc + multiply(gen_b.at[q * 2 + kh], kh)
        acc = jnp.transpose(acc)
        if q == 0:
            sib_copy.wait_recv()
        mine[q] = acc + sib[q]
        for near in (4, 8, 1, 2, 3, 5, 6, 7):
            red_copy(q, near).start()
    hints = []
    for q in range(2):
        hint = mine[q, 0:32, :]
        for near in (1, 2, 3, 5, 6, 7, 4, 8):
            red_copy(q, near).wait_recv()
        for near in range(1, 8):
            hint = hint + red[q, near]
        hints.append(hint)

    low_lane = lax.broadcasted_iota(I32, (8, 128), 1) < 64
    for t in range(4):
        for cc in range(2):
            tile_at = hints[t // 2][cc * 16 : (cc + 1) * 16, (t % 2) * 128 : (t % 2 + 1) * 128]
            top, low = tile_at[0:8, :], tile_at[8:16, :]
            hint_send[2 * t, cc] = jnp.where(low_lane, top, pltpu.roll(low, 64, 1))
            hint_send[2 * t + 1, cc] = jnp.where(low_lane, pltpu.roll(top, 64, 1), low)
    away = (zh + core) % 2
    local = away == 0
    landing = hall.at[0, pl.ds((away * 8 + y) * 8, 8), :]
    landed = r_hint.at[away * 8 + y]

    def hint_copy(dy, other):
        yy = (y + dy) % 8
        return rcopy(
            hint_send.at[yy, (core + other) % 2], landing, s_hint.at[dy * 2 + other], landed,
            dev_at(x, yy, z + away * (7 - 2 * z), (core + other) % 2),
        )

    own_hint = pltpu.make_async_copy(hint_send.at[y, core], landing, landed)
    for dy in (4, 3, 5, 2, 6, 1, 7, 0):
        for other in range(2):
            if dy or other:
                hint_copy(dy, other).start()
            else:
                @pl.when(local)
                def _():
                    own_hint.start()

                @pl.when(jnp.logical_not(local))
                def _():
                    hint_copy(0, 0).start()

    for k in range(16):
        arrived(hall.at[0, pl.ds(k * 8, 8), :], r_hint.at[k])

    def hx_copy(k):
        if k < 2:
            return rcopy(hall.at[0], hall.at[1 + 2 * k], s_hx.at[k], r_hx.at[k], dev(1 - 2 * k, 0, 0, 0))
        at = pl.ds((k - 2) * 64, 64)
        return rcopy(
            hall.at[2 * k - 3, at, :], hall.at[2, at, :], s_hx.at[k], r_hx.at[k], dev(5 - 2 * k, 0, 0, 0)
        )

    for k in range(2):
        hx_copy(k).start()

    def second(dx, total):
        turned = jnp.transpose(hall[dx])
        wide = jnp.concatenate([turned[0:64, :], turned[64:128, :]], axis=1)
        left = jnp.concatenate(
            [
                ((lax.shift_right_logical(wide, jnp.int32(8 * d)) & 255) - 128).astype(F32).astype(BF16)
                for d in range(4)
            ],
            axis=0,
        )
        lsum = lax.dot_general(left, jnp.ones((256, 128), BF16), NN, preferred_element_type=F32)
        term = joined(
            [
                lax.dot_general(left, a2[k, dx * 256 : (dx + 1) * 256, :], NN, preferred_element_type=F32)
                for k in range(4)
            ]
        )
        term = term + lsum[:, 0:1].astype(I32) * jnp.int32(BIAS)
        return term if total is None else total + term

    total = second(0, None)
    hx_copy(0).wait_recv()
    hx_copy(2).start()
    hx_copy(1).wait_recv()
    hx_copy(3).start()
    total = second(1, total)
    total = second(3, total)
    hx_copy(2).wait_recv()
    hx_copy(3).wait_recv()
    total = second(2, total)
    tot[0] = total[:, 0:128]
    tot[1] = total[:, 128:256]

    tot_copy = rcopy(tot.at[1 - core], tsib.at[0], s_tot, r_tot, sibling)
    tot_copy.start()
    tot_copy.wait_recv()
    tsib[1] = tot[core] + tsib[0]

    def z_copy(dz):
        zz = (zl + dz) % 4
        return rcopy(
            tsib.at[1, pl.ds(zz * 64, 64), :], zbuf.at[dz - 1], s_z.at[dz - 1], r_z.at[dz - 1], dev_line(dz)
        )

    for dz in (1, 3, 2):
        z_copy(dz).start()
    acc = tsib[1, pl.ds(pl.multiple_of(zl * 64, 64), 64), :]
    for dz in (1, 3, 2):
        z_copy(dz).wait_recv()
        acc = acc + zbuf[dz - 1]
    full[x, core, pl.ds(pl.multiple_of(zl * 64, 64), 64), :] = acc

    def part_of(dx, j, cc):
        return full.at[(x + 4 - dx) % 4, cc, pl.ds(((zl + 4 - j) % 4) * 64, 64), :]

    def half_of(dx, j, k):
        return full.at[(x + 4 - dx) % 4, core, pl.ds(((zl + 4 - j) % 4) * 64 + k * 32, 32), :]

    def gz_copy(dz):
        return rcopy(part_of(0, 0, core), part_of(0, 0, core), s_gz.at[dz - 1], r_gz.at[dz - 1], dev_line(dz))

    def gx_copy(j, k):
        spot = part_of(0, j, core) if k < 2 else half_of(2 * k - 3, j, k - 2)
        step = 1 - 2 * (k % 2)
        return rcopy(spot, spot, s_gx.at[j * 4 + k], r_gx.at[j * 4 + k], dev(step, 0, 0, 0))

    def gs_copy(dx, j):
        spot = part_of(dx, j, core)
        return rcopy(spot, spot, s_gs.at[dx * 4 + j], r_gs.at[dx * 4 + j], sibling)

    def out_copy(dx, cc):
        xx = (x + 4 - dx) % 4
        who = (core + cc) % 2
        return pltpu.make_async_copy(
            full.at[xx, who], out.at[:, pl.ds(xx * 256 + who * 128, 128)], s_out.at[dx * 2 + cc]
        )

    def spread(j):
        gx_copy(j, 0).start()
        gx_copy(j, 1).start()
        gs_copy(0, j).start()

    def forward(j):
        arrived(part_of(1, j, core), r_gx.at[j * 4])
        gx_copy(j, 2).start()
        gs_copy(1, j).start()
        arrived(part_of(3, j, core), r_gx.at[j * 4 + 1])
        gx_copy(j, 3).start()
        gs_copy(3, j).start()

    def finish(j):
        arrived(half_of(2, j, 0), r_gx.at[j * 4 + 2])
        arrived(half_of(2, j, 1), r_gx.at[j * 4 + 3])
        gs_copy(2, j).start()

    for dz in (2, 1, 3):
        gz_copy(dz).start()
    spread(0)
    arrived(part_of(0, 1, core), r_gz.at[0])
    spread(1)
    arrived(part_of(0, 3, core), r_gz.at[2])
    spread(3)
    forward(0)
    arrived(part_of(0, 2, core), r_gz.at[1])
    spread(2)
    out_copy(0, 0).start()
    for j in (1, 3, 2):
        forward(j)
    for dx in (1, 3):
        out_copy(dx, 0).start()
    for j in (0, 1, 3, 2):
        finish(j)
    out_copy(2, 0).start()
    for dx in (0, 1, 3, 2):
        for j in (0, 1, 3, 2):
            arrived(part_of(dx, j, 1 - core), r_gs.at[dx * 4 + j])
        out_copy(dx, 1).start()

    for near in range(8):
        for other in range(2):
            if near or other:
                ingest_copy(near, other).wait_send()
    for k in range(1, 8):
        order_copy(k).wait_send()
    sib_copy.wait_send()
    for q in range(2):
        for near in range(1, 9):
            red_copy(q, near).wait_send()
    for dy in range(8):
        for other in range(2):
            if dy or other:
                hint_copy(dy, other).wait_send()
            else:
                @pl.when(jnp.logical_not(local))
                def _():
                    hint_copy(0, 0).wait_send()
    for k in range(4):
        hx_copy(k).wait_send()
    tot_copy.wait_send()
    for d in range(1, 4):
        z_copy(d).wait_send()
        gz_copy(d).wait_send()
    for j in range(4):
        for k in range(4):
            gx_copy(j, k).wait_send()
            gs_copy(k, j).wait_send()
    for dx in range(4):
        for cc in range(2):
            out_copy(dx, cc).wait()


def on_device(ingest, row_order, matrix_seeds):
    dma = pltpu.SemaphoreType.DMA
    scratch = [
        pltpu.VMEM((256, 2048), BF16),
        pltpu.VMEM((1, 256), I32),
        pltpu.VMEM((2, 4, 8, 256), I32),
        pltpu.VMEM((1024, 16), BF16),
        pltpu.VMEM((2, 16, 2048), BF16),
        pltpu.VMEM((2, 16, 2048), BF16),
        pltpu.VMEM((4, 1024, 1024), BF16),
        pltpu.VMEM((4, 1024, 1024), BF16),
        pltpu.VMEM((2, 256, 256), I32),
        pltpu.VMEM((2, 256, 256), I32),
        pltpu.VMEM((2, 256, 256), I32),
        pltpu.VMEM((2, 8, 32, 256), I32),
        pltpu.VMEM((8, 2, 8, 128), I32),
        pltpu.VMEM((4, 128, 128), I32),
        pltpu.VMEM((4, 1024, 256), BF16),
        pltpu.VMEM((2, 256, 128), I32),
        pltpu.VMEM((2, 256, 128), I32),
        pltpu.VMEM((3, 64, 128), I32),
        pltpu.VMEM((4, 2, 256, 128), I32),
        dma((16,)), dma((16,)), dma, dma((8,)), dma((8,)), dma, dma, dma((18,)), dma((18,)), dma((16,)), dma((16,)),
        dma((4,)), dma((4,)), dma, dma, dma((3,)), dma((3,)), dma((3,)), dma((3,)), dma((16,)), dma((16,)),
        dma((16,)), dma((16,)), dma((8,)),
    ]
    total = pl.pallas_call(
        kernel,
        out_shape=jax.ShapeDtypeStruct((256, 1024), I32),
        in_specs=[
            pl.BlockSpec(memory_space=pltpu.SMEM),
            pl.BlockSpec(memory_space=pltpu.HBM),
            pl.BlockSpec(memory_space=pltpu.HBM),
        ],
        out_specs=pl.BlockSpec(memory_space=pltpu.HBM),
        scratch_shapes=scratch,
        compiler_params=pltpu.CompilerParams(
            collective_id=0, has_side_effects=True, vmem_limit_bytes=60 * 2**20
        ),
        name="hints",
    )(matrix_seeds, ingest, row_order)
    shape = (4, 2, 64, 1024)
    shift = lax.broadcasted_iota(I32, shape, 1) * 16
    halves = lax.shift_right_logical(jnp.broadcast_to(total.reshape(4, 1, 64, 1024), shape), shift) & 65535
    return halves.astype(F32) * (1.0 / 65536.0)


def solution(mesh):
    return jax.shard_map(
        on_device, mesh=mesh,
        in_specs=(P(("row", "col"), None), P("row", None), P()),
        out_specs=P(None, None, "col", None), check_vma=False,
    )
```

time: 83.6 us -> 80.8 us (0.967)
  local copies, waits for them, and re-layouts: 5.98 us -> 0 us
  Pallas kernels: 75.8 us -> 77.7 us
  other arithmetic: 1.65 us -> 2.98 us
    convert_element_type x4 -> x0, local copies, waits for them, and re-layouts: 3.42 us -> none  [the longest x2 1.71 us: on_device(): high = lax.shift_right_logical(total, jnp.int32(16)).astype(F32)]
    unnamed x6 -> x0, local copies, waits for them, and re-layouts: 2.56 us -> none
    pallas_call x1, Pallas kernels: 75.8 us -> 77.7 us  [on_device(): pl.pallas_call(kernel, out_shape=jax.ShapeDtypeStruct((256, 1024), I32),...]
    mul x1 -> x2, other arithmetic: 1.5 us -> 2.98 us  [the longest x1 2.98 us: on_device(): return halves.astype(F32) * (1.0 / 65536.0)]
where the time goes in v1:
time: 80.8 us; the launch traced here: 80.7 us
  Pallas kernels  77.7 us (96%)
  other arithmetic  2.98 us (4%)
    pallas_call x1, Pallas kernels, on_device(): pl.pallas_call(kernel, out_shape=jax.ShapeDtypeStruct((256, 1024), I32),...  77.7 us
    mul x1, other arithmetic, on_device(): return halves.astype(F32) * (1.0 / 65536.0)  2.98 us

profile of v1, /device:TPU:1, one launch (start us, length us, event | category | flops | bytes accessed | tf_op | source)
XLA Modules:
  0.0 80.7 jit_solution(3359905741859591298)
XLA Ops:
  0.0 77.7 %hints.1 = s32[256,1024]{1,0:T(8,128)} custom-call(s32[2]{0:T(128)} %seeds.1, bf16[16,32768]{1,0:T(8,128)(2,1)} %ingest.1, s32[1,256]{1,0:T(1,128)} %order.1), custom_call_target="tpu_custom_call" | custom-call | tf_op jit(solution)/shard_map/hints/pallas_call | solution.py:493
  77.7 3.0 %convert_multiply_fusion = f32[4,2,64,1024]{3,2,1,0:T(8,128)} fusion(s32[2]{0:T(128)S(1)} %iota_multiply_fusion, s32[4,64,1024]{2,1,0:T(8,128)} %bitcast.1), kind=kLoop, calls=%fused_computation | loop fusion | flops 2097152 | bytes 3145736 | tf_op jit(solution)/shard_map/mul | solution.py:511
  (1 shorter events, 0.0 us)

commit v2 on v1

--- a/solution.py
+++ b/solution.py
@@ -86,7 +86,7 @@
 def kernel(
     seeds, ingest, order, out,
     rec, order_in, orders, bdig, xdig, xdig2, gen_a, gen_b, give, sib, mine, red, hint_send, hall, a2,
-    tot, tsib, zbuf, full,
+    tot, tsib, zbuf, full, known,
     s_in, r_in, s_own, s_ord, r_ord, s_sib, r_sib, s_red, r_red, s_hint, r_hint, s_hx, r_hx, s_tot, r_tot,
     s_z, r_z, s_gz, r_gz, s_gx, r_gx, s_gs, r_gs, s_out,
 ):
@@ -119,26 +119,24 @@
 
     barrier = pltpu.get_barrier_semaphore()
 
-    def greet(device):
-        pl.semaphore_signal(barrier, inc=1, device_id=device, device_id_type=MESH)
-
-    def greet_plane(k, carry):
-        side = k // 16
-        zz = z + side * (7 - 2 * z)
-        greet(dev_at(x, (y + (k // 2) % 8) % 8, zz, (core + k) % 2))
-        return carry
-
-    lax.fori_loop(1, 32, greet_plane, 0)
-    count = 31
-    for off in ((1, 0, 0), (-1, 0, 0), (0, 0, 1), (0, 0, -1), (0, 1, 1), (0, -1, -1)):
+    def greet(device, sem):
+        pl.semaphore_signal(sem, inc=1, device_id=device, device_id_type=MESH)
+
+    count = 1
+    greet(sibling, barrier)
+    for off in ((0, 1, 0), (0, -1, 0), (1, 0, 0), (-1, 0, 0), (0, 0, 1), (0, 0, -1), (0, 1, 1), (0, -1, -1)):
         for other in range(2):
-            greet(dev(*off, other))
+            greet(dev(*off, other), barrier)
             count += 1
-    greet(dev(2, 0, 0, 0))
-    for d in range(1, 4):
-        greet(dev_line(d))
-        greet(dev_at((x + d) % 4, y, 7 - z, core))
-    pl.semaphore_wait(barrier, count + 7)
+    pl.semaphore_wait(barrier, count)
+
+    def round_send(k):
+        dx, dy, dz = ((1, 0, 0), (0, 1, 0), (0, 2, 0), (0, 0, 1), (0, 0, 2))[k]
+        greet(dev(dx, dy, dz, 0), known.at[k])
+        greet(dev(-dx, -dy, -dz, 0), known.at[k])
+
+    def round_wait(k):
+        pl.semaphore_wait(known.at[k], 2)
 
     colour = (2 * x + y + 3 * z) % 8
     sign = 1 - 2 * core
@@ -160,27 +158,14 @@
                 ingest_copy(near, other).start()
     own_in = pltpu.make_async_copy(ingest_src(0, 0), rec.at[pl.ds(core * 16, 16), :], r_in.at[core])
     own_in.start()
-
-    order_load.wait()
-    orders[0, 0] = jnp.broadcast_to(order_in[...], (8, 256))
-
-    def order_copy(k):
-        side, dx = k // 4, k % 4
-        zz = 7 - z if side else z
-        return rcopy(
-            orders.at[0, 0], orders.at[side, dx], s_ord.at[k], r_ord.at[k], dev_at((x + dx) % 4, y, zz, core)
-        )
-
-    for k in range(1, 8):
-        order_copy(k).start()
+    round_send(0)
 
     bdig[...] = jnp.transpose(column_digits(lax.broadcasted_iota(I32, (1, 1024), 1))).astype(BF16)
-    lane = lax.broadcasted_iota(I32, (1, 2048), 1)
-    mirrored = (lane // 256) % 2
-    block = ((zl + mirrored * (3 - 2 * zl)) * 4 + (x + 4 - lane // 512) % 4) * 2 + core
+    index = lax.broadcasted_iota(I32, (1, 2048), 1) + (colour * 4096 + core * 2048)
     for w in range(2):
-        xdig[w] = index_digits(lane + (colour * 4096 + core * 2048), seeds[0] + 7919 * w).astype(BF16)
-        xdig2[w] = index_digits(block * 256 + lane % 256, seeds[1] + 7919 * w).astype(BF16)
+        xdig[w] = index_digits(index, seeds[0] + 7919 * w).astype(BF16)
+    round_wait(0)
+    round_send(1)
 
     def generate(buf, t, kh):
         n_at = pl.multiple_of((((1 - core) * 2 + t) % 4) * 256, 256)
@@ -195,12 +180,71 @@
         r = lax.dot_general(buf[...], rec[:, kh * 1024 : (kh + 1) * 1024], NT, preferred_element_type=F32)
         return joined([r[k * 256 : (k + 1) * 256, :] for k in range(4)])
 
-    def ahead(t, carry):
+    for kh in range(2):
+        generate(gen_a.at[kh], 0, kh)
+    round_wait(1)
+    round_send(2)
+
+    for slot in range(16):
+        arrived(rec.at[pl.ds(slot * 16, 16), :], r_in.at[slot])
+    sums = lax.dot_general(jnp.ones((16, 2048), BF16), rec[...], NT, preferred_element_type=F32)
+    bias = sums[0:1, :].astype(I32) * jnp.int32(BIAS)
+
+    gens = (gen_a, gen_b)
+
+    def tile(t):
+        acc = bias
         for kh in range(2):
-            generate(gen_a.at[t * 2 + kh], t, kh)
-        return carry
-
-    lax.fori_loop(0, 2, ahead, 0)
+            if t < 3:
+                generate(gens[(t + 1) % 2].at[kh], t + 1, kh)
+            acc = acc + multiply(gens[t % 2].at[kh], kh)
+        return jnp.transpose(acc)
+
+    round_wait(2)
+    round_send(3)
+    give[0] = tile(0)
+    round_wait(3)
+    round_send(4)
+    give[1] = tile(1)
+    round_wait(4)
+    sib_copy = rcopy(give, sib, s_sib, r_sib, sibling)
+    sib_copy.start()
+
+    order_load.wait()
+    orders[0, 0] = jnp.broadcast_to(order_in[...], (8, 256))
+
+    def order_copy(k):
+        side, dx = k // 4, k % 4
+        zz = 7 - z if side else z
+        return rcopy(
+            orders.at[0, 0], orders.at[side, dx], s_ord.at[k], r_ord.at[k], dev_at((x + dx) % 4, y, zz, core)
+        )
+
+    for k in range(1, 8):
+        order_copy(k).start()
+
+    def red_copy(q, near):
+        if near in (4, 8):
+            at, sg = (near // 4 - 1) * 16, 1 if near == 8 else -1
+            rows, dst, device = 128 + at, red.at[q, 4, pl.ds(at, 16), :], dev(0, sg, sg, 0)
+            rows = mine.at[q, pl.ds(rows, 16), :]
+        else:
+            dx, dy, dz = NEAR[near]
+            rows, dst, device = mine.at[q, pl.ds(near * 32, 32), :], red.at[q, near], dev(-dx, -dy, -dz, 0)
+        return rcopy(rows, dst, s_red.at[q * 9 + near], r_red.at[q * 9 + near], device)
+
+    for q in range(2):
+        acc = tile(2 + q)
+        if q == 0:
+            sib_copy.wait_recv()
+        mine[q] = acc + sib[q]
+        for near in (4, 8, 1, 2, 3, 5, 6, 7):
+            red_copy(q, near).start()
+    lane = lax.broadcasted_iota(I32, (1, 2048), 1)
+    mirrored = (lane // 256) % 2
+    block = ((zl + mirrored * (3 - 2 * zl)) * 4 + (x + 4 - lane // 512) % 4) * 2 + core
+    for w in range(2):
+        xdig2[w] = index_digits(block * 256 + lane % 256, seeds[1] + 7919 * w).astype(BF16)
 
     for k in range(1, 8):
         arrived(orders.at[k // 4, k % 4], r_ord.at[k])
@@ -220,43 +264,6 @@
             a2[2 * w, dx * 256 : (dx + 1) * 256, :] = lo
             a2[2 * w + 1, dx * 256 : (dx + 1) * 256, :] = hi
 
-    for slot in range(16):
-        arrived(rec.at[pl.ds(slot * 16, 16), :], r_in.at[slot])
-    sums = lax.dot_general(jnp.ones((16, 2048), BF16), rec[...], NT, preferred_element_type=F32)
-    bias = sums[0:1, :].astype(I32) * jnp.int32(BIAS)
-
-    def tile(t, carry):
-        acc = bias
-        for kh in range(2):
-            generate(gen_b.at[t * 2 + kh], t + 2, kh)
-            acc = acc + multiply(gen_a.at[t * 2 + kh], kh)
-        give[t] = jnp.transpose(acc)
-        return carry
-
-    lax.fori_loop(0, 2, tile, 0)
-    sib_copy = rcopy(give, sib, s_sib, r_sib, sibling)
-    sib_copy.start()
-
-    def red_copy(q, near):
-        if near in (4, 8):
-            at, sg = (near // 4 - 1) * 16, 1 if near == 8 else -1
-            rows, dst, device = 128 + at, red.at[q, 4, pl.ds(at, 16), :], dev(0, sg, sg, 0)
-            rows = mine.at[q, pl.ds(rows, 16), :]
-        else:
-            dx, dy, dz = NEAR[near]
-            rows, dst, device = mine.at[q, pl.ds(near * 32, 32), :], red.at[q, near], dev(-dx, -dy, -dz, 0)
-        return rcopy(rows, dst, s_red.at[q * 9 + near], r_red.at[q * 9 + near], device)
-
-    for q in range(2):
-        acc = bias
-        for kh in range(2):
-            acc = acc + multiply(gen_b.at[q * 2 + kh], kh)
-        acc = jnp.transpose(acc)
-        if q == 0:
-            sib_copy.wait_recv()
-        mine[q] = acc + sib[q]
-        for near in (4, 8, 1, 2, 3, 5, 6, 7):
-            red_copy(q, near).start()
     hints = []
     for q in range(2):
         hint = mine[q, 0:32, :]
@@ -473,8 +480,8 @@
         pltpu.VMEM((1024, 16), BF16),
         pltpu.VMEM((2, 16, 2048), BF16),
         pltpu.VMEM((2, 16, 2048), BF16),
-        pltpu.VMEM((4, 1024, 1024), BF16),
-        pltpu.VMEM((4, 1024, 1024), BF16),
+        pltpu.VMEM((2, 1024, 1024), BF16),
+        pltpu.VMEM((2, 1024, 1024), BF16),
         pltpu.VMEM((2, 256, 256), I32),
         pltpu.VMEM((2, 256, 256), I32),
         pltpu.VMEM((2, 256, 256), I32),
@@ -486,6 +493,7 @@
         pltpu.VMEM((2, 256, 128), I32),
         pltpu.VMEM((3, 64, 128), I32),
         pltpu.VMEM((4, 2, 256, 128), I32),
+        pltpu.SemaphoreType.REGULAR((5,)),
         dma((16,)), dma((16,)), dma, dma((8,)), dma((8,)), dma, dma, dma((18,)), dma((18,)), dma((16,)), dma((16,)),
         dma((4,)), dma((4,)), dma, dma, dma((3,)), dma((3,)), dma((3,)), dma((3,)), dma((16,)), dma((16,)),
         dma((16,)), dma((16,)), dma((8,)),
@@ -505,10 +513,10 @@
         ),
         name="hints",
     )(matrix_seeds, ingest, row_order)
-    shape = (4, 2, 64, 1024)
-    shift = lax.broadcasted_iota(I32, shape, 1) * 16
-    halves = lax.shift_right_logical(jnp.broadcast_to(total.reshape(4, 1, 64, 1024), shape), shift) & 65535
-    return halves.astype(F32) * (1.0 / 65536.0)
+    total = total.reshape(4, 64, 1024)
+    low = (total & 65535).astype(F32)
+    high = lax.shift_right_logical(total, jnp.int32(16)).astype(F32)
+    return jnp.stack([low, high], axis=1) * (1.0 / 65536.0)
 
 
 def solution(mesh):

time: 80.8 us -> 75.1 us (0.929)
  Pallas kernels: 77.7 us -> 71.9 us
    pallas_call x1, Pallas kernels: 77.7 us -> 71.9 us  [on_device(): pl.pallas_call(kernel, out_shape=jax.ShapeDtypeStruct((256, 1024), I32),...]
    mul x2 -> x1, other arithmetic: 2.98 us -> 1.5 us  [on_device(): return jnp.stack([low, high], axis=1) * (1.0 / 65536.0)]
    convert_element_type x0 -> x1, other arithmetic: none -> 1.48 us  [on_device(): low = (total & 65535).astype(F32)]
where the time goes in v2:
time: 75.1 us; the launch traced here: 74.9 us
  Pallas kernels  71.9 us (96%)
  other arithmetic  2.98 us (4%)
    pallas_call x1, Pallas kernels, on_device(): pl.pallas_call(kernel, out_shape=jax.ShapeDtypeStruct((256, 1024), I32),...  71.9 us
    mul x1, other arithmetic, on_device(): return jnp.stack([low, high], axis=1) * (1.0 / 65536.0)  1.5 us

profile of v2, /device:TPU:1, one launch (start us, length us, event | category | flops | bytes accessed | tf_op | source)
XLA Modules:
  0.0 74.9 jit_solution(16889443479476549967)
XLA Ops:
  0.0 71.9 %hints.1 = s32[256,1024]{1,0:T(8,128)} custom-call(s32[2]{0:T(128)} %seeds.1, bf16[16,32768]{1,0:T(8,128)(2,1)} %ingest.1, s32[1,256]{1,0:T(1,128)} %order.1), custom_call_target="tpu_custom_call" | custom-call | tf_op jit(solution)/shard_map/hints/pallas_call | solution.py:501
  71.9 1.5 %and_convert_fusion = (f32[256,1024]{1,0:T(8,128)S(1)}, f32[256,1024]{1,0:T(8,128)S(1)}) fusion(s32[256,1024]{1,0:T(8,128)} %hints.1), kind=kLoop, calls=%fused_computation.2 | loop fusion | flops 1048576 | bytes 3145728 | tf_op jit(solution)/shard_map/convert_element_type | solution.py:517
  73.4 1.5 %maximum_multiply_fusion = f32[4,2,64,1024]{3,2,1,0:T(8,128)} fusion(f32[4,1,64,1024]{3,2,1,0:T(8,128)S(1)} %bitcast.7, f32[4,1,64,1024]{3,2,1,0:T(8,128)S(1)} %bitcast.6), kind=kLoop, calls=%fused_computation | loop fusion | flops 1048576 | bytes 4194304 | tf_op jit(solution)/shard_map/mul | solution.py:519

commit v3 on v2

--- a/solution.py
+++ b/solution.py
@@ -86,7 +86,7 @@
 def kernel(
     seeds, ingest, order, out,
     rec, order_in, orders, bdig, xdig, xdig2, gen_a, gen_b, give, sib, mine, red, hint_send, hall, a2,
-    tot, tsib, zbuf, full, known,
+    tot, tsib, zbuf, full, fbuf, known,
     s_in, r_in, s_own, s_ord, r_ord, s_sib, r_sib, s_red, r_red, s_hint, r_hint, s_hx, r_hx, s_tot, r_tot,
     s_z, r_z, s_gz, r_gz, s_gx, r_gx, s_gs, r_gs, s_out,
 ):
@@ -254,7 +254,8 @@
     wanted = ingest_row + 256 * side
     lane = lax.broadcasted_iota(I32, (1, 512), 1)
     quarter = bdig[pl.ds(pl.multiple_of(x * 256, 256), 256), :]
-    for dx in range(4):
+
+    def second_rows(dx):
         have = jnp.concatenate([orders[0, dx, 0:1, :], orders[1, dx, 0:1, :]], axis=1) + (lane // 256) * 256
         onehot = (wanted == have).astype(F32).astype(BF16)
         for w in range(2):
@@ -264,6 +265,8 @@
             a2[2 * w, dx * 256 : (dx + 1) * 256, :] = lo
             a2[2 * w + 1, dx * 256 : (dx + 1) * 256, :] = hi
 
+    second_rows(0)
+    second_rows(1)
     hints = []
     for q in range(2):
         hint = mine[q, 0:32, :]
@@ -306,6 +309,8 @@
                 def _():
                     hint_copy(0, 0).start()
 
+    second_rows(3)
+    second_rows(2)
     for k in range(16):
         arrived(hall.at[0, pl.ds(k * 8, 8), :], r_hint.at[k])
 
@@ -386,34 +391,40 @@
         step = 1 - 2 * (k % 2)
         return rcopy(spot, spot, s_gx.at[j * 4 + k], r_gx.at[j * 4 + k], dev(step, 0, 0, 0))
 
+    def out_at(dx, j, cc):
+        return out.at[(zl + 4 - j) % 4, :, :, pl.ds(((x + 4 - dx) % 4) * 256 + cc * 128, 128)]
+
     def gs_copy(dx, j):
-        spot = part_of(dx, j, core)
-        return rcopy(spot, spot, s_gs.at[dx * 4 + j], r_gs.at[dx * 4 + j], sibling)
-
-    def out_copy(dx, cc):
-        xx = (x + 4 - dx) % 4
-        who = (core + cc) % 2
-        return pltpu.make_async_copy(
-            full.at[xx, who], out.at[:, pl.ds(xx * 256 + who * 128, 128)], s_out.at[dx * 2 + cc]
-        )
+        k = dx * 4 + j
+        return rcopy(fbuf.at[dx, j], out_at(dx, j, core), s_gs.at[k], r_gs.at[k], sibling)
+
+    def out_copy(dx, j):
+        return pltpu.make_async_copy(fbuf.at[dx, j], out_at(dx, j, core), s_out.at[dx * 4 + j])
+
+    def emit(dx, j):
+        value = full[(x + 4 - dx) % 4, core, pl.ds(pl.multiple_of(((zl + 4 - j) % 4) * 64, 64), 64), :]
+        fbuf[dx, j, 0] = (value & 65535).astype(F32) * (1.0 / 65536.0)
+        fbuf[dx, j, 1] = lax.shift_right_logical(value, jnp.int32(16)).astype(F32) * (1.0 / 65536.0)
+        gs_copy(dx, j).start()
+        out_copy(dx, j).start()
 
     def spread(j):
         gx_copy(j, 0).start()
         gx_copy(j, 1).start()
-        gs_copy(0, j).start()
+        emit(0, j)
 
     def forward(j):
         arrived(part_of(1, j, core), r_gx.at[j * 4])
         gx_copy(j, 2).start()
-        gs_copy(1, j).start()
         arrived(part_of(3, j, core), r_gx.at[j * 4 + 1])
         gx_copy(j, 3).start()
-        gs_copy(3, j).start()
+        emit(1, j)
+        emit(3, j)
 
     def finish(j):
         arrived(half_of(2, j, 0), r_gx.at[j * 4 + 2])
         arrived(half_of(2, j, 1), r_gx.at[j * 4 + 3])
-        gs_copy(2, j).start()
+        emit(2, j)
 
     for dz in (2, 1, 3):
         gz_copy(dz).start()
@@ -425,18 +436,13 @@
     forward(0)
     arrived(part_of(0, 2, core), r_gz.at[1])
     spread(2)
-    out_copy(0, 0).start()
     for j in (1, 3, 2):
         forward(j)
-    for dx in (1, 3):
-        out_copy(dx, 0).start()
     for j in (0, 1, 3, 2):
         finish(j)
-    out_copy(2, 0).start()
     for dx in (0, 1, 3, 2):
         for j in (0, 1, 3, 2):
-            arrived(part_of(dx, j, 1 - core), r_gs.at[dx * 4 + j])
-        out_copy(dx, 1).start()
+            arrived(out_at(dx, j, 1 - core), r_gs.at[dx * 4 + j])
 
     for near in range(8):
         for other in range(2):
@@ -467,8 +473,8 @@
             gx_copy(j, k).wait_send()
             gs_copy(k, j).wait_send()
     for dx in range(4):
-        for cc in range(2):
-            out_copy(dx, cc).wait()
+        for j in range(4):
+            out_copy(dx, j).wait()
 
 
 def on_device(ingest, row_order, matrix_seeds):
@@ -493,14 +499,15 @@
         pltpu.VMEM((2, 256, 128), I32),
         pltpu.VMEM((3, 64, 128), I32),
         pltpu.VMEM((4, 2, 256, 128), I32),
+        pltpu.VMEM((4, 4, 2, 64, 128), F32),
         pltpu.SemaphoreType.REGULAR((5,)),
         dma((16,)), dma((16,)), dma, dma((8,)), dma((8,)), dma, dma, dma((18,)), dma((18,)), dma((16,)), dma((16,)),
         dma((4,)), dma((4,)), dma, dma, dma((3,)), dma((3,)), dma((3,)), dma((3,)), dma((16,)), dma((16,)),
-        dma((16,)), dma((16,)), dma((8,)),
+        dma((16,)), dma((16,)), dma((16,)),
     ]
-    total = pl.pallas_call(
+    return pl.pallas_call(
         kernel,
-        out_shape=jax.ShapeDtypeStruct((256, 1024), I32),
+        out_shape=jax.ShapeDtypeStruct((4, 2, 64, 1024), F32),
         in_specs=[
             pl.BlockSpec(memory_space=pltpu.SMEM),
             pl.BlockSpec(memory_space=pltpu.HBM),
@@ -513,10 +520,6 @@
         ),
         name="hints",
     )(matrix_seeds, ingest, row_order)
-    total = total.reshape(4, 64, 1024)
-    low = (total & 65535).astype(F32)
-    high = lax.shift_right_logical(total, jnp.int32(16)).astype(F32)
-    return jnp.stack([low, high], axis=1) * (1.0 / 65536.0)
 
 
 def solution(mesh):

time: 75.1 us -> 75 us (level)
  local copies, waits for them, and re-layouts: 0 us -> 3.16 us
  other arithmetic: 2.98 us -> 0 us
    unnamed x0 -> x1, local copies, waits for them, and re-layouts: none -> 3.16 us
    mul x1 -> x0, other arithmetic: 1.5 us -> none  [on_device(): return jnp.stack([low, high], axis=1) * (1.0 / 65536.0)]
    convert_element_type x1 -> x0, other arithmetic: 1.48 us -> none  [on_device(): low = (total & 65535).astype(F32)]
where the time goes in v3:
time: 75 us; the launch traced here: 74.9 us
  Pallas kernels  71.7 us (96%)
  local copies, waits for them, and re-layouts  3.16 us (4%)
    pallas_call x1, Pallas kernels, on_device(): pl.pallas_call(kernel, out_shape=jax.ShapeDtypeStruct((4, 2, 64, 1024), F...  71.7 us
    unnamed x1, local copies, waits for them, and re-layouts  3.16 us

profile of v3, /device:TPU:1, one launch (start us, length us, event | category | flops | bytes accessed | tf_op | source)
XLA Modules:
  0.0 74.9 jit_solution(14598915476442446422)
XLA Ops:
  0.0 71.7 %hints.1 = f32[4,2,64,1024]{3,2,1,0:T(8,128)} custom-call(s32[2]{0:T(128)} %seeds.1, bf16[16,32768]{1,0:T(8,128)(2,1)} %ingest.1, s32[1,256]{1,0:T(1,128)} %order.1), custom_call_target="tpu_custom_call" | custom-call | tf_op jit(solution)/shard_map/hints/pallas_call | solution.py:508
  71.7 3.2 %copy.5 = f32[4,2,64,1024]{3,2,1,0:T(8,128)} copy(f32[4,2,64,1024]{3,2,1,0:T(8,128)} %hints.1) | data formatting | bytes 4194304

commit v4 on v3

--- a/solution.py
+++ b/solution.py
@@ -86,7 +86,7 @@
 def kernel(
     seeds, ingest, order, out,
     rec, order_in, orders, bdig, xdig, xdig2, gen_a, gen_b, give, sib, mine, red, hint_send, hall, a2,
-    tot, tsib, zbuf, full, fbuf, known,
+    tot, tsib, zbuf, full, known,
     s_in, r_in, s_own, s_ord, r_ord, s_sib, r_sib, s_red, r_red, s_hint, r_hint, s_hx, r_hx, s_tot, r_tot,
     s_z, r_z, s_gz, r_gz, s_gx, r_gx, s_gs, r_gs, s_out,
 ):
@@ -392,19 +392,16 @@
         return rcopy(spot, spot, s_gx.at[j * 4 + k], r_gx.at[j * 4 + k], dev(step, 0, 0, 0))
 
     def out_at(dx, j, cc):
-        return out.at[(zl + 4 - j) % 4, :, :, pl.ds(((x + 4 - dx) % 4) * 256 + cc * 128, 128)]
+        return out.at[pl.ds(((zl + 4 - j) % 4) * 64, 64), pl.ds(((x + 4 - dx) % 4) * 256 + cc * 128, 128)]
 
     def gs_copy(dx, j):
         k = dx * 4 + j
-        return rcopy(fbuf.at[dx, j], out_at(dx, j, core), s_gs.at[k], r_gs.at[k], sibling)
+        return rcopy(part_of(dx, j, core), out_at(dx, j, core), s_gs.at[k], r_gs.at[k], sibling)
 
     def out_copy(dx, j):
-        return pltpu.make_async_copy(fbuf.at[dx, j], out_at(dx, j, core), s_out.at[dx * 4 + j])
+        return pltpu.make_async_copy(part_of(dx, j, core), out_at(dx, j, core), s_out.at[dx * 4 + j])
 
     def emit(dx, j):
-        value = full[(x + 4 - dx) % 4, core, pl.ds(pl.multiple_of(((zl + 4 - j) % 4) * 64, 64), 64), :]
-        fbuf[dx, j, 0] = (value & 65535).astype(F32) * (1.0 / 65536.0)
-        fbuf[dx, j, 1] = lax.shift_right_logical(value, jnp.int32(16)).astype(F32) * (1.0 / 65536.0)
         gs_copy(dx, j).start()
         out_copy(dx, j).start()
 
@@ -426,22 +423,20 @@
         arrived(half_of(2, j, 1), r_gx.at[j * 4 + 3])
         emit(2, j)
 
+    close = 3 - 2 * (zl // 2)
+    chunks = (0, close, 2, 4 - close)
     for dz in (2, 1, 3):
         gz_copy(dz).start()
     spread(0)
-    arrived(part_of(0, 1, core), r_gz.at[0])
-    spread(1)
-    arrived(part_of(0, 3, core), r_gz.at[2])
-    spread(3)
-    forward(0)
-    arrived(part_of(0, 2, core), r_gz.at[1])
-    spread(2)
-    for j in (1, 3, 2):
-        forward(j)
-    for j in (0, 1, 3, 2):
+    for k in range(1, 4):
+        arrived(part_of(0, chunks[k], core), r_gz.at[chunks[k] - 1])
+        spread(chunks[k])
+        forward(chunks[k - 1])
+    forward(chunks[3])
+    for j in chunks:
         finish(j)
-    for dx in (0, 1, 3, 2):
-        for j in (0, 1, 3, 2):
+    for dx in range(4):
+        for j in range(4):
             arrived(out_at(dx, j, 1 - core), r_gs.at[dx * 4 + j])
 
     for near in range(8):
@@ -477,6 +472,12 @@
             out_copy(dx, j).wait()
 
 
+def halves(total, out):
+    value = total[...]
+    out[0, 0] = (value & 65535).astype(F32) * (1.0 / 65536.0)
+    out[0, 1] = lax.shift_right_logical(value, jnp.int32(16)).astype(F32) * (1.0 / 65536.0)
+
+
 def on_device(ingest, row_order, matrix_seeds):
     dma = pltpu.SemaphoreType.DMA
     scratch = [
@@ -499,15 +500,14 @@
         pltpu.VMEM((2, 256, 128), I32),
         pltpu.VMEM((3, 64, 128), I32),
         pltpu.VMEM((4, 2, 256, 128), I32),
-        pltpu.VMEM((4, 4, 2, 64, 128), F32),
         pltpu.SemaphoreType.REGULAR((5,)),
         dma((16,)), dma((16,)), dma, dma((8,)), dma((8,)), dma, dma, dma((18,)), dma((18,)), dma((16,)), dma((16,)),
         dma((4,)), dma((4,)), dma, dma, dma((3,)), dma((3,)), dma((3,)), dma((3,)), dma((16,)), dma((16,)),
         dma((16,)), dma((16,)), dma((16,)),
     ]
-    return pl.pallas_call(
+    total = pl.pallas_call(
         kernel,
-        out_shape=jax.ShapeDtypeStruct((4, 2, 64, 1024), F32),
+        out_shape=jax.ShapeDtypeStruct((256, 1024), I32),
         in_specs=[
             pl.BlockSpec(memory_space=pltpu.SMEM),
             pl.BlockSpec(memory_space=pltpu.HBM),
@@ -520,6 +520,14 @@
         ),
         name="hints",
     )(matrix_seeds, ingest, row_order)
+    return pl.pallas_call(
+        halves,
+        grid=(4,),
+        out_shape=jax.ShapeDtypeStruct((4, 2, 64, 1024), F32),
+        in_specs=[pl.BlockSpec((64, 1024), lambda d: (d, 0))],
+        out_specs=pl.BlockSpec((1, 2, 64, 1024), lambda d: (d, 0, 0, 0)),
+        name="halves",
+    )(total)
 
 
 def solution(mesh):

time: 75 us -> 75.1 us (level)
  Pallas kernels: 71.7 us -> 74.9 us
  local copies, waits for them, and re-layouts: 3.16 us -> 0 us
    pallas_call x1 -> x2, Pallas kernels: 71.7 us -> 74.9 us  [the longest x1 71.3 us: on_device(): pl.pallas_call(kernel, out_shape=jax.ShapeDtypeStruct((256, 1024), I32),...]
    unnamed x1 -> x0, local copies, waits for them, and re-layouts: 3.16 us -> none
where the time goes in v4:
time: 75.1 us; the launch traced here: 74.9 us
  Pallas kernels  74.9 us (100%)
    pallas_call x1, Pallas kernels, on_device(): pl.pallas_call(kernel, out_shape=jax.ShapeDtypeStruct((256, 1024), I32),...  71.3 us
    pallas_call x1, Pallas kernels, on_device(): pl.pallas_call(halves, grid=(4,), out_shape=jax.ShapeDtypeStruct((4, 2, 6...  3.62 us

profile of v4, /device:TPU:1, one launch (start us, length us, event | category | flops | bytes accessed | tf_op | source)
XLA Modules:
  0.0 74.9 jit_solution(4731500075125650754)
XLA Ops:
  0.0 71.3 %hints.1.total = s32[256,1024]{1,0:T(8,128)} custom-call(s32[2]{0:T(128)} %seeds.1, bf16[16,32768]{1,0:T(8,128)(2,1)} %ingest.1, s32[1,256]{1,0:T(1,128)} %order.1), custom_call_target="tpu_custom_call" | custom-call | tf_op jit(solution)/shard_map/hints/pallas_call | solution.py:508
  71.3 3.6 %halves.1 = f32[4,2,64,1024]{3,2,1,0:T(8,128)} custom-call(s32[256,1024]{1,0:T(8,128)} %hints.1.total), custom_call_target="tpu_custom_call" | custom-call | tf_op jit(solution)/shard_map/halves/pallas_call | solution.py:523

commit v5 on v4

--- a/solution.py
+++ b/solution.py
@@ -470,12 +470,6 @@
     for dx in range(4):
         for j in range(4):
             out_copy(dx, j).wait()
-
-
-def halves(total, out):
-    value = total[...]
-    out[0, 0] = (value & 65535).astype(F32) * (1.0 / 65536.0)
-    out[0, 1] = lax.shift_right_logical(value, jnp.int32(16)).astype(F32) * (1.0 / 65536.0)
 
 
 def on_device(ingest, row_order, matrix_seeds):
@@ -520,14 +514,10 @@
         ),
         name="hints",
     )(matrix_seeds, ingest, row_order)
-    return pl.pallas_call(
-        halves,
-        grid=(4,),
-        out_shape=jax.ShapeDtypeStruct((4, 2, 64, 1024), F32),
-        in_specs=[pl.BlockSpec((64, 1024), lambda d: (d, 0))],
-        out_specs=pl.BlockSpec((1, 2, 64, 1024), lambda d: (d, 0, 0, 0)),
-        name="halves",
-    )(total)
+    total = total.reshape(4, 64, 1024)
+    low = (total & 65535).astype(F32)
+    high = lax.shift_right_logical(total, jnp.int32(16)).astype(F32)
+    return jnp.stack([low, high], axis=1) * (1.0 / 65536.0)
 
 
 def solution(mesh):

time: 75.1 us -> 74.4 us (level)
  Pallas kernels: 74.9 us -> 71.3 us
  other arithmetic: 0 us -> 2.98 us
    pallas_call x1 -> x0, Pallas kernels: 3.62 us -> none  [on_device(): pl.pallas_call(halves, grid=(4,), out_shape=jax.ShapeDtypeStruct((4, 2, 6...]
    mul x0 -> x1, other arithmetic: none -> 1.5 us  [on_device(): return jnp.stack([low, high], axis=1) * (1.0 / 65536.0)]
    convert_element_type x0 -> x1, other arithmetic: none -> 1.48 us  [on_device(): low = (total & 65535).astype(F32)]
where the time goes in v5:
time: 74.4 us; the launch traced here: 74.3 us
  Pallas kernels  71.3 us (96%)
  other arithmetic  2.98 us (4%)
    pallas_call x1, Pallas kernels, on_device(): pl.pallas_call(kernel, out_shape=jax.ShapeDtypeStruct((256, 1024), I32),...  71.3 us
    mul x1, other arithmetic, on_device(): return jnp.stack([low, high], axis=1) * (1.0 / 65536.0)  1.5 us

profile of v5, /device:TPU:1, one launch (start us, length us, event | category | flops | bytes accessed | tf_op | source)
XLA Modules:
  0.0 74.3 jit_solution(9475898141551210066)
XLA Ops:
  0.0 71.3 %hints.1 = s32[256,1024]{1,0:T(8,128)} custom-call(s32[2]{0:T(128)} %seeds.1, bf16[16,32768]{1,0:T(8,128)(2,1)} %ingest.1, s32[1,256]{1,0:T(1,128)} %order.1), custom_call_target="tpu_custom_call" | custom-call | tf_op jit(solution)/shard_map/hints/pallas_call | solution.py:502
  71.3 1.5 %and_convert_fusion = (f32[256,1024]{1,0:T(8,128)S(1)}, f32[256,1024]{1,0:T(8,128)S(1)}) fusion(s32[256,1024]{1,0:T(8,128)} %hints.1), kind=kLoop, calls=%fused_computation.2 | loop fusion | flops 1048576 | bytes 3145728 | tf_op jit(solution)/shard_map/convert_element_type | solution.py:518
  72.8 1.5 %maximum_multiply_fusion = f32[4,2,64,1024]{3,2,1,0:T(8,128)} fusion(f32[4,1,64,1024]{3,2,1,0:T(8,128)S(1)} %bitcast.7, f32[4,1,64,1024]{3,2,1,0:T(8,128)S(1)} %bitcast.6), kind=kLoop, calls=%fused_computation | loop fusion | flops 1048576 | bytes 4194304 | tf_op jit(solution)/shard_map/mul | solution.py:520

commit v6 on v5

--- a/solution.py
+++ b/solution.py
@@ -182,6 +182,7 @@
 
     for kh in range(2):
         generate(gen_a.at[kh], 0, kh)
+    generate(gen_b.at[0], 1, 0)
     round_wait(1)
     round_send(2)
 
@@ -195,7 +196,7 @@
     def tile(t):
         acc = bias
         for kh in range(2):
-            if t < 3:
+            if t < 3 and (t or kh):
                 generate(gens[(t + 1) % 2].at[kh], t + 1, kh)
             acc = acc + multiply(gens[t % 2].at[kh], kh)
         return jnp.transpose(acc)

time: 74.4 us -> 74.2 us (level)
  no operation moved by 1% of the time
where the time goes in v6:
time: 74.2 us; the launch traced here: 74.1 us
  Pallas kernels  71.1 us (96%)
  other arithmetic  2.98 us (4%)
    pallas_call x1, Pallas kernels, on_device(): pl.pallas_call(kernel, out_shape=jax.ShapeDtypeStruct((256, 1024), I32),...  71.1 us
    mul x1, other arithmetic, on_device(): return jnp.stack([low, high], axis=1) * (1.0 / 65536.0)  1.5 us

profile of v6, /device:TPU:1, one launch (start us, length us, event | category | flops | bytes accessed | tf_op | source)
XLA Modules:
  0.0 74.1 jit_solution(17074770976638897374)
XLA Ops:
  0.0 71.1 %hints.1 = s32[256,1024]{1,0:T(8,128)} custom-call(s32[2]{0:T(128)} %seeds.1, bf16[16,32768]{1,0:T(8,128)(2,1)} %ingest.1, s32[1,256]{1,0:T(1,128)} %order.1), custom_call_target="tpu_custom_call" | custom-call | tf_op jit(solution)/shard_map/hints/pallas_call | solution.py:503
  71.1 1.5 %and_convert_fusion = (f32[256,1024]{1,0:T(8,128)S(1)}, f32[256,1024]{1,0:T(8,128)S(1)}) fusion(s32[256,1024]{1,0:T(8,128)} %hints.1), kind=kLoop, calls=%fused_computation.2 | loop fusion | flops 1048576 | bytes 3145728 | tf_op jit(solution)/shard_map/convert_element_type | solution.py:519
  72.6 1.5 %maximum_multiply_fusion = f32[4,2,64,1024]{3,2,1,0:T(8,128)} fusion(f32[4,1,64,1024]{3,2,1,0:T(8,128)S(1)} %bitcast.7, f32[4,1,64,1024]{3,2,1,0:T(8,128)S(1)} %bitcast.6), kind=kLoop, calls=%fused_computation | loop fusion | flops 1048576 | bytes 4194304 | tf_op jit(solution)/shard_map/mul | solution.py:521
